TPU v7x, 512 devices: a whole 4x8x8 slice. The times are simulated.
512 devices in a mesh: dp: 8 (over z), expert: 64 (over x, y, core).
Axes of the slice: x: 4, y: 8, z: 8, core: 2. Of those that a mesh axis runs over, the one named last changes fastest.
Arguments:
- tokens: bfloat16 [2048, 2048], P('expert', 'dp'), may hold values from -6 to 6
- cotangent: bfloat16 [2048, 2048], P('expert', 'dp'), may hold values from -6 to 6
- routes: int32 [2048, 8], P('expert'), may hold values from 0 to 63, all different within a row; in each aligned block of 32 rows (0 to 31, 32 to 63, ...) at most 5 rows name the same one
- probs: float32 [2048, 8], P('expert'), may hold values from 0.03 to 0.6
- matching: int32 [64], replicated, may hold values from 0 to 63, as said below
- gate_weight: bfloat16 [64, 2048, 1024], P('expert', None, 'dp'), may hold values from -0.125 to 0.125
- up_weight: bfloat16 [64, 2048, 1024], P('expert', None, 'dp'), may hold values from -0.125 to 0.125
- down_weight: bfloat16 [64, 2048, 1024], P('expert', None, 'dp'), may hold values from -0.1875 to 0.1875
Outputs:
- input_grad: bfloat16 [2048, 2048], P('expert', 'dp')
- gate_weight_grad: float32 [64, 2048, 1024], P('expert', None, 'dp')
- up_weight_grad: float32 [64, 2048, 1024], P('expert', None, 'dp')
- down_weight_grad: float32 [64, 2048, 1024], P('expert', None, 'dp')
Inputs may be any that keep to these rules, and one draw needn't show every extreme that they name: matching pairs the experts: matching[matching[i]] == i and matching[i] != i. `routes`: each token names 8 different experts; within each aligned block of 32 tokens no expert is named by more than 5 tokens.
All inputs are finite; a program needn't handle non-finite values.
Results may differ from a plain program's by a relative error of at most 0.015.
Values may be sent and summed in bfloat16 or wider, within the bound.
No kernel may reach another device: no remote copies, remote signals or barrier semaphores. Data moves between devices by JAX's collectives and lax.ppermute only.
A program may use at most 64 MiB of HBM per device.

v0:
```python
import jax
import jax.numpy as jnp
from jax import lax
from jax.sharding import PartitionSpec as P

contract_rows = (((0,), (0,)), ((), ()))
contract_cols = (((1,), (1,)), ((), ()))


def relay_weights(first, second, third):
    return (
        lax.all_to_all(first, "expert", split_axis=1, concat_axis=0, tiled=True),
        lax.all_to_all(second, "expert", split_axis=1, concat_axis=0, tiled=True),
        lax.all_to_all(third, "expert", split_axis=1, concat_axis=0, tiled=True),
    )


def migrate(arrays, matching, mover):
    experts = matching.shape[0]
    model_width = arrays[0].shape[-2]
    hidden_width = arrays[0].shape[-1]
    piece_rows = model_width // experts
    split = [a.reshape(1, experts, piece_rows, hidden_width) for a in arrays]
    spread = mover(split[0], split[1], split[2])
    ordered = [
        jnp.take(s, matching, axis=0).reshape(1, experts, piece_rows, hidden_width) for s in spread
    ]
    landed = mover(ordered[0], ordered[1], ordered[2])
    return [w.reshape(model_width, hidden_width) for w in landed]


def layout(routes, probs, target_table, capacity):
    experts = target_table.shape[0]
    tok_rows = routes.shape[0]
    top_count = routes.shape[1]
    pair_count = tok_rows * top_count
    pair_expert = routes.reshape(pair_count)
    onehot = (pair_expert[:, None] == jnp.arange(experts, dtype=jnp.int32)[None, :]).astype(
        jnp.int32
    )
    running = jnp.cumsum(onehot, axis=0)
    rank = jnp.sum(onehot * running, axis=1) - 1
    target = jnp.sum(onehot * target_table[None, :], axis=1)
    slot = target * capacity + rank
    slot_total = experts * capacity
    owners = jnp.arange(pair_count, dtype=jnp.int32) // top_count
    slot_token = jnp.full((slot_total,), tok_rows, jnp.int32).at[slot].set(owners)
    slot_prob = jnp.zeros((slot_total,), jnp.float32).at[slot].set(probs.reshape(pair_count))
    return (slot, slot_token, slot_prob)


def build_rows(tokens, cotangent, slot_token, slot_prob):
    blank = jnp.zeros((1, tokens.shape[1]), jnp.bfloat16)
    inputs = jnp.take(jnp.concatenate([tokens, blank], axis=0), slot_token, axis=0)
    picked = jnp.take(jnp.concatenate([cotangent, blank], axis=0), slot_token, axis=0)
    grads = (picked.astype(jnp.float32) * slot_prob[:, None]).astype(jnp.bfloat16)
    return (inputs, grads)


def combine_pairs(returned, slot, tok_rows, top_count):
    rows = jnp.take(returned, slot, axis=0)
    return jnp.sum(rows.reshape(tok_rows, top_count, returned.shape[1]), axis=1)


def expert_grads(inputs, grads, w_gate, w_up, w_down):
    gate = jnp.dot(inputs, w_gate, preferred_element_type=jnp.float32)
    upper = jnp.dot(inputs, w_up, preferred_element_type=jnp.float32)
    sig = jax.nn.sigmoid(gate)
    hidden = (gate * sig * upper).astype(jnp.bfloat16)
    hidden_back = jnp.dot(grads, w_down, preferred_element_type=jnp.float32)
    up_back = (hidden_back * gate * sig).astype(jnp.bfloat16)
    gate_back = (hidden_back * upper * sig * (1.0 + gate * (1.0 - sig))).astype(jnp.bfloat16)
    gate_sum = lax.dot_general(inputs, gate_back, contract_rows, preferred_element_type=jnp.float32)
    up_sum = lax.dot_general(inputs, up_back, contract_rows, preferred_element_type=jnp.float32)
    down_sum = lax.dot_general(grads, hidden, contract_rows, preferred_element_type=jnp.float32)
    return (gate_sum, up_sum, down_sum, gate_back, up_back)


def slice_back(gate_back, up_back, w_gate, w_up):
    first = lax.dot_general(gate_back, w_gate, contract_cols, preferred_element_type=jnp.float32)
    return first + lax.dot_general(up_back, w_up, contract_cols, preferred_element_type=jnp.float32)


def local(tokens, cotangent, routes, probs, matching, gate_weight, up_weight, down_weight):
    experts = matching.shape[0]
    tok_rows = routes.shape[0]
    top_count = routes.shape[1]
    capacity = max(2, 5 * tok_rows * top_count // (4 * experts))
    model_width = gate_weight.shape[1]
    hidden_width = gate_weight.shape[2]
    w_gate, w_up, w_down = migrate((gate_weight, up_weight, down_weight), matching, relay_weights)
    slot, slot_token, slot_prob = layout(routes, probs, matching, capacity)
    whole_in, whole_out = (
        lax.all_gather(tokens, "dp", axis=1, tiled=True),
        lax.all_gather(cotangent, "dp", axis=1, tiled=True),
    )
    inputs, grads = build_rows(whole_in, whole_out, slot_token, slot_prob)
    arrived_in, arrived_out = (
        lax.all_to_all(inputs, "expert", split_axis=0, concat_axis=0, tiled=True),
        lax.all_to_all(grads, "expert", split_axis=0, concat_axis=0, tiled=True),
    )
    gate_sum, up_sum, down_sum, gate_back, up_back = expert_grads(
        arrived_in, arrived_out, w_gate, w_up, w_down
    )
    partial_value = slice_back(gate_back, up_back, w_gate, w_up).astype(jnp.bfloat16)
    pair_back = lax.psum_scatter(partial_value, "dp", scatter_dimension=1, tiled=True).astype(
        jnp.float32
    )
    returned = lax.all_to_all(
        pair_back.astype(jnp.bfloat16), "expert", split_axis=0, concat_axis=0, tiled=True
    ).astype(pair_back.dtype)
    token_sum = combine_pairs(returned, slot, tok_rows, top_count)
    return (
        token_sum.astype(jnp.bfloat16),
        gate_sum.reshape(1, model_width, hidden_width),
        up_sum.reshape(1, model_width, hidden_width),
        down_sum.reshape(1, model_width, hidden_width),
    )


def solution(mesh):
    placed = (
        P("expert", "dp"),
        P("expert", "dp"),
        P("expert", None),
        P("expert", None),
        P(),
        P("expert", None, "dp"),
        P("expert", None, "dp"),
        P("expert", None, "dp"),
    )
    return jax.shard_map(
        local,
        mesh=mesh,
        in_specs=placed,
        out_specs=(
            P("expert", "dp"),
            P("expert", None, "dp"),
            P("expert", None, "dp"),
            P("expert", None, "dp"),
        ),
        check_vma=False,
    )
```

profile of v0, /device:TPU:1, one launch (start us, length us, event | category | flops | bytes accessed | tf_op | source)
XLA Modules:
  0.0 365.6 jit_solution(9097960822106262097)
XLA Ops:
  7.2 29.1 %all_to_all.96 = bf16[1,64,32,128]{3,2,0,1:T(8,128)(2,1)S(1)} all-to-all(bf16[1,64,32,128]{3,2,0,1:T(8,128)(2,1)} %bitcast.85), channel_id=1, replica_groups=mesh['dp'=8,'expert'=64] {'expert'}, dimensions={1} | all-to-all | bytes 1048576 | tf_op jit(solution)/shard_map/all_to_all | solution.py:13
  36.3 23.5 %all_to_all.97 = bf16[1,64,32,128]{3,2,0,1:T(8,128)(2,1)S(1)} all-to-all(bf16[1,64,32,128]{3,2,0,1:T(8,128)(2,1)S(1)} %bitcast.86), channel_id=1, replica_groups=mesh['dp'=8,'expert'=64] {'expert'}, dimensions={1} | all-to-all | bytes 1048576 | tf_op jit(solution)/shard_map/all_to_all | solution.py:12
  59.8 6.3 %all-to-all-start.1 = ((bf16[1,64,32,128]{3,2,0,1:T(8,128)(2,1)}), bf16[1,64,32,128]{3,2,0,1:T(8,128)(2,1)S(1)}, u32[]{:S(2)}, u32[]{:S(2)}) async-start(bf16[1,64,32,128]{3,2,0,1:T(8,128)(2,1)} %bitcast.3), calls=%async_computation.1 | async-start | bytes 1048576 | tf_op jit(solution)/shard_map/all_to_all | solution.py:14
  67.7 15.7 %all-to-all-done.1 = bf16[1,64,32,128]{3,2,0,1:T(8,128)(2,1)S(1)} async-done(((bf16[1,64,32,128]{3,2,0,1:T(8,128)(2,1)}), bf16[1,64,32,128]{3,2,0,1:T(8,128)(2,1)S(1)}, u32[]{:S(2)}, u32[]{:S(2)}) %all-to-all-start.1) | async-done | bytes 524320 | tf_op jit(solution)/shard_map/all_to_all | solution.py:14
  84.1 1.4 fusion.2
  85.4 6.4 %all-to-all-start.7 = ((bf16[1,64,32,128]{3,2,0,1:T(8,128)(2,1)}), bf16[1,64,32,128]{3,2,0,1:T(8,128)(2,1)S(1)}, u32[]{:S(2)}, u32[]{:S(2)}) async-start(bf16[1,64,32,128]{3,2,0,1:T(8,128)(2,1)} %get-tuple-element.11), calls=%async_computation.7 | async-start | bytes 1048576 | tf_op jit(solution)/shard_map/all_to_all | solution.py:12
  92.7 26.1 %all_gather.7 = bf16[32,2048]{1,0:T(8,128)(2,1)S(1)} all-gather(bf16[32,256]{1,0:T(8,128)(2,1)S(1)} %copy-done.8), channel_id=1, replica_groups=mesh['dp'=8,'expert'=64] {'dp'}, dimensions={1}, use_global_device_ids=true | all-gather | bytes 147456 | tf_op jit(solution)/shard_map/all_gather | solution.py:94
  119.5 1.4 scatter_custom_fusion
  120.9 15.2 %all-to-all-start.5 = ((bf16[1,64,32,128]{3,2,0,1:T(8,128)(2,1)}), bf16[1,64,32,128]{3,2,0,1:T(8,128)(2,1)S(1)}, u32[]{:S(2)}, u32[]{:S(2)}) async-start(bf16[1,64,32,128]{3,2,0,1:T(8,128)(2,1)} %get-tuple-element.10), calls=%async_computation.5 | async-start | bytes 1048576 | tf_op jit(solution)/shard_map/all_to_all | solution.py:13
  136.1 2.4 gather_fusion.3
  138.8 1.6 all_to_all.76
  140.4 13.0 %all-to-all-done.5 = bf16[1,64,32,128]{3,2,0,1:T(8,128)(2,1)S(1)} async-done(((bf16[1,64,32,128]{3,2,0,1:T(8,128)(2,1)}), bf16[1,64,32,128]{3,2,0,1:T(8,128)(2,1)S(1)}, u32[]{:S(2)}, u32[]{:S(2)}) %all-to-all-start.5) | async-done | bytes 524320 | tf_op jit(solution)/shard_map/all_to_all | solution.py:13
  154.2 6.3 %all-to-all-start.3 = ((bf16[64,5,2048]{2,1,0:T(8,128)(2,1)}), bf16[64,5,2048]{2,1,0:T(8,128)(2,1)S(1)}, u32[]{:S(2)}, u32[]{:S(2)}) async-start(bf16[64,5,2048]{2,1,0:T(8,128)(2,1)} %all_to_all.76), calls=%async_computation.3 | async-start | bytes 4194304 | tf_op jit(solution)/shard_map/all_to_all | solution.py:99
  160.5 20.2 %all_gather.6 = bf16[32,2048]{1,0:T(8,128)(2,1)S(1)} all-gather(bf16[32,256]{1,0:T(8,128)(2,1)S(1)} %copy-done.9), channel_id=1, replica_groups=mesh['dp'=8,'expert'=64] {'dp'}, dimensions={1}, use_global_device_ids=true | all-gather | bytes 147456 | tf_op jit(solution)/shard_map/all_gather | solution.py:95
  180.8 3.0 gather_fusion.1
  184.0 1.6 scatter_custom_fusion.1
  185.6 1.7 multiply_convert_fusion
  187.3 1.6 all_to_all.70
  188.9 22.9 %all-to-all-done.3 = bf16[64,5,2048]{2,1,0:T(8,128)(2,1)S(1)} async-done(((bf16[64,5,2048]{2,1,0:T(8,128)(2,1)}), bf16[64,5,2048]{2,1,0:T(8,128)(2,1)S(1)}, u32[]{:S(2)}, u32[]{:S(2)}) %all-to-all-start.3) | async-done | bytes 1310752 | tf_op jit(solution)/shard_map/all_to_all | solution.py:99
  211.8 57.2 %all_to_all.98 = bf16[64,5,2048]{2,1,0:T(8,128)(2,1)} all-to-all(bf16[64,5,2048]{2,1,0:T(8,128)(2,1)} %all_to_all.70), channel_id=1, replica_groups=mesh['dp'=8,'expert'=64] {'expert'}, dimensions={0} | all-to-all | bytes 2621440 | tf_op jit(solution)/shard_map/all_to_all | solution.py:100
  268.9 6.0 %all-to-all-start.2 = ((bf16[1,64,32,128]{3,2,0,1:T(8,128)(2,1)}), bf16[1,64,32,128]{3,2,0,1:T(8,128)(2,1)}, u32[]{:S(2)}, u32[]{:S(2)}) async-start(bf16[1,64,32,128]{3,2,0,1:T(8,128)(2,1)} %get-tuple-element.12), calls=%async_computation.2 | async-start | bytes 1048576 | tf_op jit(solution)/shard_map/all_to_all | solution.py:14
  275.6 2.6 all_to_all.72
  279.8 12.4 %all-to-all-done.2 = bf16[1,64,32,128]{3,2,0,1:T(8,128)(2,1)} async-done(((bf16[1,64,32,128]{3,2,0,1:T(8,128)(2,1)}), bf16[1,64,32,128]{3,2,0,1:T(8,128)(2,1)}, u32[]{:S(2)}, u32[]{:S(2)}) %all-to-all-start.2) | async-done | bytes 524320 | tf_op jit(solution)/shard_map/all_to_all | solution.py:14
  292.2 1.5 multiply_convert_fusion.2
  294.8 1.6 fusion
  297.2 1.6 convolution_bitcast_fusion.2
  298.8 30.0 %reduce-scatter.2.cloned.1.call-done = bf16[320,256]{1,0:T(8,128)(2,1)} async-done(((bf16[320,2048]{1,0:T(8,128)(2,1)}), bf16[320,256]{1,0:T(8,128)(2,1)}) %reduce-scatter.2.cloned.1.call-update) | async-done | bytes 163856 | tf_op jit(solution)/shard_map/reduce_scatter | solution.py:106
  328.8 1.7 all_to_all.85
  330.5 14.4 %all-to-all-start.8 = ((bf16[64,5,256]{2,1,0:T(8,128)(2,1)}), bf16[64,5,256]{2,1,0:T(8,128)(2,1)S(1)}, u32[]{:S(2)}, u32[]{:S(2)}) async-start(bf16[64,5,256]{2,1,0:T(8,128)(2,1)} %all_to_all.85), calls=%async_computation.9 | async-start | bytes 524288 | tf_op jit(solution)/shard_map/all_to_all | solution.py:109
  345.0 1.6 convolution_bitcast_fusion.1
  346.6 1.6 convolution_bitcast_fusion
  348.2 8.8 %all-to-all-done.8 = bf16[64,5,256]{2,1,0:T(8,128)(2,1)S(1)} async-done(((bf16[64,5,256]{2,1,0:T(8,128)(2,1)}), bf16[64,5,256]{2,1,0:T(8,128)(2,1)S(1)}, u32[]{:S(2)}, u32[]{:S(2)}) %all-to-all-start.8) | async-done | bytes 163872 | tf_op jit(solution)/shard_map/all_to_all | solution.py:109
  (73 shorter events, 10.8 us)
Async XLA Ops:
  7.2 29.1 %copy-start.5 = (bf16[1,2048,128]{2,1,0:T(8,128)(2,1)S(1)}, bf16[1,2048,128]{2,1,0:T(8,128)(2,1)}, u32[]{:S(2)}) copy-start(bf16[1,2048,128]{2,1,0:T(8,128)(2,1)} %param.17) | copy-start | bytes 1572868
  36.3 29.8 %copy-start.12 = (s32[32,8]{0,1:T(8,128)S(1)}, s32[32,8]{0,1:T(8,128)}, u32[]{:S(2)}) copy-start(s32[32,8]{0,1:T(8,128)} %param.14) | copy-start | bytes 3076
  36.3 30.1 %copy-start.16 = (s32[64]{0:T(128)S(1)}, s32[64]{0:T(128)}, u32[]{:S(2)}) copy-start(s32[64]{0:T(128)} %param.16) | copy-start | bytes 772
  59.8 23.6 %all-to-all-start.1 = ((bf16[1,64,32,128]{3,2,0,1:T(8,128)(2,1)}), bf16[1,64,32,128]{3,2,0,1:T(8,128)(2,1)S(1)}, u32[]{:S(2)}, u32[]{:S(2)}) async-start(bf16[1,64,32,128]{3,2,0,1:T(8,128)(2,1)} %bitcast.3), calls=%async_computation.1 | async-start | bytes 1048576 | tf_op jit(solution)/shard_map/all_to_all | solution.py:14
  85.4 7.3 %copy-start.8 = (bf16[32,256]{1,0:T(8,128)(2,1)S(1)}, bf16[32,256]{1,0:T(8,128)(2,1)}, u32[]{:S(2)}) copy-start(bf16[32,256]{1,0:T(8,128)(2,1)} %param.12) | copy-start | bytes 49156
  85.4 35.5 %all-to-all-start.7 = ((bf16[1,64,32,128]{3,2,0,1:T(8,128)(2,1)}), bf16[1,64,32,128]{3,2,0,1:T(8,128)(2,1)S(1)}, u32[]{:S(2)}, u32[]{:S(2)}) async-start(bf16[1,64,32,128]{3,2,0,1:T(8,128)(2,1)} %get-tuple-element.11), calls=%async_computation.7 | async-start | bytes 1048576 | tf_op jit(solution)/shard_map/all_to_all | solution.py:12
  118.9 0.6 copy-start.10
  119.5 64.5 %copy-start.14 = (s32[256,1]{0,1:T(1,128)}, s32[256,1]{0,1:T(1,128)S(1)}, u32[]{:S(2)}) copy-start(s32[256,1]{0,1:T(1,128)S(1)} %compare_select_fusion.1) | copy-start | bytes 3076
  120.9 15.2 %copy-start = (bf16[1,64,32,128]{3,2,0,1:T(8,128)(2,1)}, bf16[1,64,32,128]{3,2,0,1:T(8,128)(2,1)S(1)}, u32[]{:S(2)}) copy-start(bf16[1,64,32,128]{3,2,0,1:T(8,128)(2,1)S(1)} %all-to-all-done.7) | copy-start | bytes 1572868
  120.9 32.5 %all-to-all-start.5 = ((bf16[1,64,32,128]{3,2,0,1:T(8,128)(2,1)}), bf16[1,64,32,128]{3,2,0,1:T(8,128)(2,1)S(1)}, u32[]{:S(2)}, u32[]{:S(2)}) async-start(bf16[1,64,32,128]{3,2,0,1:T(8,128)(2,1)} %get-tuple-element.10), calls=%async_computation.5 | async-start | bytes 1048576 | tf_op jit(solution)/shard_map/all_to_all | solution.py:13
  140.4 20.1 %copy-start.9 = (bf16[32,256]{1,0:T(8,128)(2,1)S(1)}, bf16[32,256]{1,0:T(8,128)(2,1)}, u32[]{:S(2)}) copy-start(bf16[32,256]{1,0:T(8,128)(2,1)} %param.13) | copy-start | bytes 49156
  153.4 0.8 copy-start.2
  154.2 57.5 %all-to-all-start.3 = ((bf16[64,5,2048]{2,1,0:T(8,128)(2,1)}), bf16[64,5,2048]{2,1,0:T(8,128)(2,1)S(1)}, u32[]{:S(2)}, u32[]{:S(2)}) async-start(bf16[64,5,2048]{2,1,0:T(8,128)(2,1)} %all_to_all.76), calls=%async_computation.3 | async-start | bytes 4194304 | tf_op jit(solution)/shard_map/all_to_all | solution.py:99
  180.8 3.0 copy-start.13
  268.9 23.3 %all-to-all-start.2 = ((bf16[1,64,32,128]{3,2,0,1:T(8,128)(2,1)}), bf16[1,64,32,128]{3,2,0,1:T(8,128)(2,1)}, u32[]{:S(2)}, u32[]{:S(2)}) async-start(bf16[1,64,32,128]{3,2,0,1:T(8,128)(2,1)} %get-tuple-element.12), calls=%async_computation.2 | async-start | bytes 1048576 | tf_op jit(solution)/shard_map/all_to_all | solution.py:14
  274.9 53.9 %reduce-scatter.2.cloned.1.call-start = ((), (), s32[]{:S(2)}) async-start(), calls=%async_computation.10 | async-start | bytes 1474560 | tf_op jit(solution)/shard_map/reduce_scatter | solution.py:106
  275.6 2.7 copy-start.1
  278.2 1.0 copy-start.3
  293.7 0.6 copy-start.6
  293.7 1.1 copy-start.4
  296.4 0.7 copy-start.11
  296.4 0.7 copy-start.15
  297.2 47.8 %copy-start.7 = (bf16[320,128]{1,0:T(8,128)(2,1)S(1)}, bf16[320,128]{1,0:T(8,128)(2,1)}, u32[]{:S(2)}) copy-start(bf16[320,128]{1,0:T(8,128)(2,1)} %copy-done.6) | copy-start | bytes 245764
  330.5 26.4 %all-to-all-start.8 = ((bf16[64,5,256]{2,1,0:T(8,128)(2,1)}), bf16[64,5,256]{2,1,0:T(8,128)(2,1)S(1)}, u32[]{:S(2)}, u32[]{:S(2)}) async-start(bf16[64,5,256]{2,1,0:T(8,128)(2,1)} %all_to_all.85), calls=%async_computation.9 | async-start | bytes 524288 | tf_op jit(solution)/shard_map/all_to_all | solution.py:109
Sparse Core Ops, SparseCore 0:
  296.6 32.2 reduce-scatter.1
where the time goes:
time: 367 us; the launch traced here: 366 us
  blocking collectives  156 us (43%)
  waiting for transfers between devices  103 us (28%)
  starting transfers between devices  54.6 us (15%)
  local copies, waits for them, and re-layouts  23.3 us (6%)
  between operations  14.4 us (4%)
  matrix products  9.48 us (3%)
  other arithmetic  4.82 us (1%)
    all_to_all x1, blocking collectives, local(): lax.all_to_all(grads, 'expert', split_axis=0, concat_axis=0, tiled=True)  57.2 us
    reduce_scatter x1, waiting for transfers between devices, local(): lax.psum_scatter(partial_value, 'dp', scatter_dimension=1, tiled=True)  30 us
    all_to_all x1, blocking collectives, relay_weights(): lax.all_to_all(second, 'expert', split_axis=1, concat_axis=0, tiled=True)  29.1 us
    all_to_all x2, waiting for transfers between devices, relay_weights(): lax.all_to_all(third, 'expert', split_axis=1, concat_axis=0, tiled=True)  28.1 us
    all_gather x1, blocking collectives, local(): lax.all_gather(tokens, 'dp', axis=1, tiled=True)  26.1 us
    all_to_all x1, blocking collectives, relay_weights(): lax.all_to_all(first, 'expert', split_axis=1, concat_axis=0, tiled=True)  23.5 us
    all_to_all x1, waiting for transfers between devices, local(): lax.all_to_all(inputs, 'expert', split_axis=0, concat_axis=0, tiled=True)  22.9 us
    all_gather x1, blocking collectives, local(): lax.all_gather(cotangent, 'dp', axis=1, tiled=True)  20.2 us
  transfers between devices with their start and end apart: 7, of which 6 were waited for; matrix products, arithmetic and copies ran while one was open for 5% of the time, Pallas kernels for 0%

commit v1 on v0

--- a/solution.py
+++ b/solution.py
@@ -5,6 +5,14 @@
 
 contract_rows = (((0,), (0,)), ((), ()))
 contract_cols = (((1,), (1,)), ((), ()))
+
+
+def gather_by_exchange(shard, axis, dim):
+    size = lax.axis_size(axis)
+    repeats = [size if d == dim else 1 for d in range(shard.ndim)]
+    return lax.all_to_all(
+        jnp.tile(shard, repeats), axis, split_axis=dim, concat_axis=dim, tiled=True
+    )
 
 
 def relay_weights(first, second, third):
@@ -91,7 +99,7 @@
     w_gate, w_up, w_down = migrate((gate_weight, up_weight, down_weight), matching, relay_weights)
     slot, slot_token, slot_prob = layout(routes, probs, matching, capacity)
     whole_in, whole_out = (
-        lax.all_gather(tokens, "dp", axis=1, tiled=True),
+        gather_by_exchange(tokens, "dp", 1),
         lax.all_gather(cotangent, "dp", axis=1, tiled=True),
     )
     inputs, grads = build_rows(whole_in, whole_out, slot_token, slot_prob)

time: 367 us -> 377 us (1.027)
  blocking collectives: 156 us -> 129 us
  waiting for transfers between devices: 103 us -> 128 us
  starting transfers between devices: 54.6 us -> 66.3 us
    all_to_all x1 -> x2, waiting for transfers between devices: 22.9 us -> 51 us  [the longest x1 45.1 us: local(): lax.all_to_all(grads, 'expert', split_axis=0, concat_axis=0, tiled=True)]
    all_gather x1 -> x0, blocking collectives: 26.1 us -> none  [local(): lax.all_gather(tokens, 'dp', axis=1, tiled=True)]
    all_to_all x1 -> x2, starting transfers between devices: 6.28 us -> 16.3 us  [the longest x1 10 us: gather_by_exchange(): lax.all_to_all(jnp.tile(shard, repeats), axis, split_axis=dim, concat_axi...]
  transfers between devices with their start and end apart: 7 -> 8, of which waited for: 6 -> 7; matrix products, arithmetic and copies ran while one was open for 5% -> 6% of each run, Pallas kernels for 0% -> 0%
where the time goes in v1:
time: 377 us; the launch traced here: 376 us
  blocking collectives  129 us (34%)
  waiting for transfers between devices  128 us (34%)
  starting transfers between devices  66.3 us (18%)
  local copies, waits for them, and re-layouts  23.3 us (6%)
  between operations  14.5 us (4%)
  matrix products  9.46 us (3%)
  other arithmetic  4.82 us (1%)
    all_to_all x1, blocking collectives, local(): lax.all_to_all(inputs, 'expert', split_axis=0, concat_axis=0, tiled=True)  57.2 us
    all_to_all x1, waiting for transfers between devices, local(): lax.all_to_all(grads, 'expert', split_axis=0, concat_axis=0, tiled=True)  45.1 us
    all_to_all x1, blocking collectives, relay_weights(): lax.all_to_all(second, 'expert', split_axis=1, concat_axis=0, tiled=True)  29.1 us
    reduce_scatter x1, waiting for transfers between devices, local(): lax.psum_scatter(partial_value, 'dp', scatter_dimension=1, tiled=True)  28.8 us
    all_to_all x2, waiting for transfers between devices, relay_weights(): lax.all_to_all(third, 'expert', split_axis=1, concat_axis=0, tiled=True)  28.1 us
    all_to_all x1, blocking collectives, relay_weights(): lax.all_to_all(first, 'expert', split_axis=1, concat_axis=0, tiled=True)  23.5 us
    all_gather x1, blocking collectives, local(): lax.all_gather(cotangent, 'dp', axis=1, tiled=True)  19.7 us
    all_to_all x1, starting transfers between devices, relay_weights(): lax.all_to_all(second, 'expert', split_axis=1, concat_axis=0, tiled=True)  15.2 us
  transfers between devices with their start and end apart: 8, of which 7 were waited for; matrix products, arithmetic and copies ran while one was open for 6% of the time, Pallas kernels for 0%

profile of v1, /device:TPU:1, one launch (start us, length us, event | category | flops | bytes accessed | tf_op | source)
XLA Modules:
  0.0 375.9 jit_solution(1189057560015589617)
XLA Ops:
  7.2 29.1 %all_to_all.105 = bf16[1,64,32,128]{3,2,0,1:T(8,128)(2,1)S(1)} all-to-all(bf16[1,64,32,128]{3,2,0,1:T(8,128)(2,1)} %bitcast.87), channel_id=1, replica_groups=mesh['dp'=8,'expert'=64] {'expert'}, dimensions={1} | all-to-all | bytes 1048576 | tf_op jit(solution)/shard_map/all_to_all | solution.py:21
  36.3 23.5 %all_to_all.106 = bf16[1,64,32,128]{3,2,0,1:T(8,128)(2,1)S(1)} all-to-all(bf16[1,64,32,128]{3,2,0,1:T(8,128)(2,1)S(1)} %bitcast.88), channel_id=1, replica_groups=mesh['dp'=8,'expert'=64] {'expert'}, dimensions={1} | all-to-all | bytes 1048576 | tf_op jit(solution)/shard_map/all_to_all | solution.py:20
  59.8 6.3 %all-to-all-start.1 = ((bf16[1,64,32,128]{3,2,0,1:T(8,128)(2,1)}), bf16[1,64,32,128]{3,2,0,1:T(8,128)(2,1)S(1)}, u32[]{:S(2)}, u32[]{:S(2)}) async-start(bf16[1,64,32,128]{3,2,0,1:T(8,128)(2,1)} %bitcast.3), calls=%async_computation.1 | async-start | bytes 1048576 | tf_op jit(solution)/shard_map/all_to_all | solution.py:22
  67.7 15.7 %all-to-all-done.1 = bf16[1,64,32,128]{3,2,0,1:T(8,128)(2,1)S(1)} async-done(((bf16[1,64,32,128]{3,2,0,1:T(8,128)(2,1)}), bf16[1,64,32,128]{3,2,0,1:T(8,128)(2,1)S(1)}, u32[]{:S(2)}, u32[]{:S(2)}) %all-to-all-start.1) | async-done | bytes 524320 | tf_op jit(solution)/shard_map/all_to_all | solution.py:22
  84.1 10.0 %all-to-all-start.3 = ((bf16[32,8,256]{2,0,1:T(8,128)(2,1)}), bf16[32,8,256]{2,0,1:T(8,128)(2,1)S(1)}, u32[]{:S(2)}, u32[]{:S(2)}) async-start(bf16[32,8,256]{2,0,1:T(8,128)(2,1)} %tile.2), calls=%async_computation.3 | async-start | bytes 262144 | tf_op jit(solution)/shard_map/all_to_all | solution.py:13
  96.1 6.0 %all-to-all-done.3 = bf16[32,8,256]{2,0,1:T(8,128)(2,1)S(1)} async-done(((bf16[32,8,256]{2,0,1:T(8,128)(2,1)}), bf16[32,8,256]{2,0,1:T(8,128)(2,1)S(1)}, u32[]{:S(2)}, u32[]{:S(2)}) %all-to-all-start.3) | async-done | bytes 131104 | tf_op jit(solution)/shard_map/all_to_all | solution.py:13
  102.1 7.7 %all-to-all-start.8 = ((bf16[1,64,32,128]{3,2,0,1:T(8,128)(2,1)}), bf16[1,64,32,128]{3,2,0,1:T(8,128)(2,1)S(1)}, u32[]{:S(2)}, u32[]{:S(2)}) async-start(bf16[1,64,32,128]{3,2,0,1:T(8,128)(2,1)} %get-tuple-element.11), calls=%async_computation.8 | async-start | bytes 1048576 | tf_op jit(solution)/shard_map/all_to_all | solution.py:20
  110.8 19.7 %all_gather.3 = bf16[32,2048]{1,0:T(8,128)(2,1)S(1)} all-gather(bf16[32,256]{1,0:T(8,128)(2,1)S(1)} %copy-done.9), channel_id=1, replica_groups=mesh['dp'=8,'expert'=64] {'dp'}, dimensions={1}, use_global_device_ids=true | all-gather | bytes 147456 | tf_op jit(solution)/shard_map/all_gather | solution.py:103
  130.7 1.4 scatter_custom_fusion
  132.1 15.2 %all-to-all-start.6 = ((bf16[1,64,32,128]{3,2,0,1:T(8,128)(2,1)}), bf16[1,64,32,128]{3,2,0,1:T(8,128)(2,1)S(1)}, u32[]{:S(2)}, u32[]{:S(2)}) async-start(bf16[1,64,32,128]{3,2,0,1:T(8,128)(2,1)} %get-tuple-element.10), calls=%async_computation.6 | async-start | bytes 1048576 | tf_op jit(solution)/shard_map/all_to_all | solution.py:21
  147.4 2.4 gather_fusion.1
  149.8 1.4 scatter_custom_fusion.1
  151.6 1.6 all_to_all.76
  153.2 11.4 %all-to-all-done.6 = bf16[1,64,32,128]{3,2,0,1:T(8,128)(2,1)S(1)} async-done(((bf16[1,64,32,128]{3,2,0,1:T(8,128)(2,1)}), bf16[1,64,32,128]{3,2,0,1:T(8,128)(2,1)S(1)}, u32[]{:S(2)}, u32[]{:S(2)}) %all-to-all-start.6) | async-done | bytes 524320 | tf_op jit(solution)/shard_map/all_to_all | solution.py:21
  165.4 6.3 %all-to-all-start = ((bf16[64,5,2048]{2,1,0:T(8,128)(2,1)}), bf16[64,5,2048]{2,1,0:T(8,128)(2,1)S(1)}, u32[]{:S(2)}, u32[]{:S(2)}) async-start(bf16[64,5,2048]{2,1,0:T(8,128)(2,1)} %all_to_all.76), calls=%async_computation | async-start | bytes 4194304 | tf_op jit(solution)/shard_map/all_to_all | solution.py:108
  171.8 3.0 gather_fusion.3
  174.8 1.5 broadcast_select_fusion
  176.3 1.6 all_to_all.84
  177.9 45.1 %all-to-all-done = bf16[64,5,2048]{2,1,0:T(8,128)(2,1)S(1)} async-done(((bf16[64,5,2048]{2,1,0:T(8,128)(2,1)}), bf16[64,5,2048]{2,1,0:T(8,128)(2,1)S(1)}, u32[]{:S(2)}, u32[]{:S(2)}) %all-to-all-start) | async-done | bytes 1310752 | tf_op jit(solution)/shard_map/all_to_all | solution.py:108
  223.0 57.2 %all_to_all.107 = bf16[64,5,2048]{2,1,0:T(8,128)(2,1)} all-to-all(bf16[64,5,2048]{2,1,0:T(8,128)(2,1)} %all_to_all.84), channel_id=1, replica_groups=mesh['dp'=8,'expert'=64] {'expert'}, dimensions={0} | all-to-all | bytes 2621440 | tf_op jit(solution)/shard_map/all_to_all | solution.py:107
  280.1 6.0 %all-to-all-start.2 = ((bf16[1,64,32,128]{3,2,0,1:T(8,128)(2,1)}), bf16[1,64,32,128]{3,2,0,1:T(8,128)(2,1)}, u32[]{:S(2)}, u32[]{:S(2)}) async-start(bf16[1,64,32,128]{3,2,0,1:T(8,128)(2,1)} %get-tuple-element.12), calls=%async_computation.2 | async-start | bytes 1048576 | tf_op jit(solution)/shard_map/all_to_all | solution.py:22
  286.8 2.6 all_to_all.86
  291.0 12.4 %all-to-all-done.2 = bf16[1,64,32,128]{3,2,0,1:T(8,128)(2,1)} async-done(((bf16[1,64,32,128]{3,2,0,1:T(8,128)(2,1)}), bf16[1,64,32,128]{3,2,0,1:T(8,128)(2,1)}, u32[]{:S(2)}, u32[]{:S(2)}) %all-to-all-start.2) | async-done | bytes 524320 | tf_op jit(solution)/shard_map/all_to_all | solution.py:22
  303.4 1.5 multiply_convert_fusion.2
  306.0 1.6 fusion
  308.4 1.6 convolution_bitcast_fusion.2
  310.0 28.8 %reduce-scatter.2.cloned.1.call-done = bf16[320,256]{1,0:T(8,128)(2,1)} async-done(((bf16[320,2048]{1,0:T(8,128)(2,1)}), bf16[320,256]{1,0:T(8,128)(2,1)}) %reduce-scatter.2.cloned.1.call-update) | async-done | bytes 163856 | tf_op jit(solution)/shard_map/reduce_scatter | solution.py:114
  338.8 1.7 all_to_all.93
  340.5 14.7 %all-to-all-start.9 = ((bf16[64,5,256]{2,1,0:T(8,128)(2,1)}), bf16[64,5,256]{2,1,0:T(8,128)(2,1)S(1)}, u32[]{:S(2)}, u32[]{:S(2)}) async-start(bf16[64,5,256]{2,1,0:T(8,128)(2,1)} %all_to_all.93), calls=%async_computation.10 | async-start | bytes 524288 | tf_op jit(solution)/shard_map/all_to_all | solution.py:117
  355.3 1.6 convolution_bitcast_fusion.1
  356.9 1.6 convolution_bitcast_fusion
  358.5 8.8 %all-to-all-done.9 = bf16[64,5,256]{2,1,0:T(8,128)(2,1)S(1)} async-done(((bf16[64,5,256]{2,1,0:T(8,128)(2,1)}), bf16[64,5,256]{2,1,0:T(8,128)(2,1)S(1)}, u32[]{:S(2)}, u32[]{:S(2)}) %all-to-all-start.9) | async-done | bytes 163872 | tf_op jit(solution)/shard_map/all_to_all | solution.py:117
  (76 shorter events, 12.5 us)
Async XLA Ops:
  7.2 29.1 %copy-start.5 = (bf16[1,2048,128]{2,1,0:T(8,128)(2,1)S(1)}, bf16[1,2048,128]{2,1,0:T(8,128)(2,1)}, u32[]{:S(2)}) copy-start(bf16[1,2048,128]{2,1,0:T(8,128)(2,1)} %param.17) | copy-start | bytes 1572868
  36.3 29.8 %copy-start.12 = (s32[32,8]{0,1:T(8,128)S(1)}, s32[32,8]{0,1:T(8,128)}, u32[]{:S(2)}) copy-start(s32[32,8]{0,1:T(8,128)} %param.14) | copy-start | bytes 3076
  36.3 30.1 %copy-start.16 = (s32[64]{0:T(128)S(1)}, s32[64]{0:T(128)}, u32[]{:S(2)}) copy-start(s32[64]{0:T(128)} %param.16) | copy-start | bytes 772
  59.8 23.6 %all-to-all-start.1 = ((bf16[1,64,32,128]{3,2,0,1:T(8,128)(2,1)}), bf16[1,64,32,128]{3,2,0,1:T(8,128)(2,1)S(1)}, u32[]{:S(2)}, u32[]{:S(2)}) async-start(bf16[1,64,32,128]{3,2,0,1:T(8,128)(2,1)} %bitcast.3), calls=%async_computation.1 | async-start | bytes 1048576 | tf_op jit(solution)/shard_map/all_to_all | solution.py:22
  66.1 17.3 %copy-start.8 = (bf16[32,256]{1,0:T(8,128)(2,1)S(1)}, bf16[32,256]{1,0:T(8,128)(2,1)}, u32[]{:S(2)}) copy-start(bf16[32,256]{1,0:T(8,128)(2,1)} %param.12) | copy-start | bytes 49156
  84.1 18.0 %all-to-all-start.3 = ((bf16[32,8,256]{2,0,1:T(8,128)(2,1)}), bf16[32,8,256]{2,0,1:T(8,128)(2,1)S(1)}, u32[]{:S(2)}, u32[]{:S(2)}) async-start(bf16[32,8,256]{2,0,1:T(8,128)(2,1)} %tile.2), calls=%async_computation.3 | async-start | bytes 262144 | tf_op jit(solution)/shard_map/all_to_all | solution.py:13
  96.1 14.5 %copy-start.13 = (f32[32,8]{0,1:T(8,128)S(1)}, f32[32,8]{0,1:T(8,128)}, u32[]{:S(2)}) copy-start(f32[32,8]{0,1:T(8,128)} %param.15) | copy-start | bytes 3076
  96.1 14.7 %copy-start.9 = (bf16[32,256]{1,0:T(8,128)(2,1)S(1)}, bf16[32,256]{1,0:T(8,128)(2,1)}, u32[]{:S(2)}) copy-start(bf16[32,256]{1,0:T(8,128)(2,1)} %param.13) | copy-start | bytes 49156
  102.1 30.0 %all-to-all-start.8 = ((bf16[1,64,32,128]{3,2,0,1:T(8,128)(2,1)}), bf16[1,64,32,128]{3,2,0,1:T(8,128)(2,1)S(1)}, u32[]{:S(2)}, u32[]{:S(2)}) async-start(bf16[1,64,32,128]{3,2,0,1:T(8,128)(2,1)} %get-tuple-element.11), calls=%async_computation.8 | async-start | bytes 1048576 | tf_op jit(solution)/shard_map/all_to_all | solution.py:20
  130.6 16.7 %copy-start.10 = (s32[256]{0:T(256)}, s32[256]{0:T(256)S(1)}, u32[]{:S(2)}) copy-start(s32[256]{0:T(256)S(1)} %add_add_fusion) | copy-start | bytes 3076
  130.6 19.2 %copy-start.14 = (s32[256,1]{0,1:T(1,128)}, s32[256,1]{0,1:T(1,128)S(1)}, u32[]{:S(2)}) copy-start(s32[256,1]{0,1:T(1,128)S(1)} %compare_select_fusion.1) | copy-start | bytes 3076
  132.1 15.3 %copy-start = (bf16[1,64,32,128]{3,2,0,1:T(8,128)(2,1)}, bf16[1,64,32,128]{3,2,0,1:T(8,128)(2,1)S(1)}, u32[]{:S(2)}) copy-start(bf16[1,64,32,128]{3,2,0,1:T(8,128)(2,1)S(1)} %all-to-all-done.8) | copy-start | bytes 1572868
  132.1 32.6 %all-to-all-start.6 = ((bf16[1,64,32,128]{3,2,0,1:T(8,128)(2,1)}), bf16[1,64,32,128]{3,2,0,1:T(8,128)(2,1)S(1)}, u32[]{:S(2)}, u32[]{:S(2)}) async-start(bf16[1,64,32,128]{3,2,0,1:T(8,128)(2,1)} %get-tuple-element.10), calls=%async_computation.6 | async-start | bytes 1048576 | tf_op jit(solution)/shard_map/all_to_all | solution.py:21
  164.6 0.8 copy-start.2
  165.4 57.5 %all-to-all-start = ((bf16[64,5,2048]{2,1,0:T(8,128)(2,1)}), bf16[64,5,2048]{2,1,0:T(8,128)(2,1)S(1)}, u32[]{:S(2)}, u32[]{:S(2)}) async-start(bf16[64,5,2048]{2,1,0:T(8,128)(2,1)} %all_to_all.76), calls=%async_computation | async-start | bytes 4194304 | tf_op jit(solution)/shard_map/all_to_all | solution.py:108
  280.1 23.3 %all-to-all-start.2 = ((bf16[1,64,32,128]{3,2,0,1:T(8,128)(2,1)}), bf16[1,64,32,128]{3,2,0,1:T(8,128)(2,1)}, u32[]{:S(2)}, u32[]{:S(2)}) async-start(bf16[1,64,32,128]{3,2,0,1:T(8,128)(2,1)} %get-tuple-element.12), calls=%async_computation.2 | async-start | bytes 1048576 | tf_op jit(solution)/shard_map/all_to_all | solution.py:22
  286.2 52.7 %reduce-scatter.2.cloned.1.call-start = ((), (), s32[]{:S(2)}) async-start(), calls=%async_computation.11 | async-start | bytes 1474560 | tf_op jit(solution)/shard_map/reduce_scatter | solution.py:114
  286.8 2.7 copy-start.1
  289.4 1.0 copy-start.3
  304.9 0.6 copy-start.6
  305.0 1.1 copy-start.4
  307.6 0.7 copy-start.11
  307.6 0.8 copy-start.15
  308.4 46.8 %copy-start.7 = (bf16[320,128]{1,0:T(8,128)(2,1)S(1)}, bf16[320,128]{1,0:T(8,128)(2,1)}, u32[]{:S(2)}) copy-start(bf16[320,128]{1,0:T(8,128)(2,1)} %copy-done.6) | copy-start | bytes 245764
  340.5 26.8 %all-to-all-start.9 = ((bf16[64,5,256]{2,1,0:T(8,128)(2,1)}), bf16[64,5,256]{2,1,0:T(8,128)(2,1)S(1)}, u32[]{:S(2)}, u32[]{:S(2)}) async-start(bf16[64,5,256]{2,1,0:T(8,128)(2,1)} %all_to_all.93), calls=%async_computation.10 | async-start | bytes 524288 | tf_op jit(solution)/shard_map/all_to_all | solution.py:117
Sparse Core Ops, SparseCore 0:
  307.8 30.9 reduce-scatter.1
